TPU v7x, 32 devices: a whole 2x2x4 slice. The times are simulated.
32 devices in a mesh: section: 2 (over y), dp: 16 (over z, x, core).
Axes of the slice: x: 2, y: 2, z: 4, core: 2. Of those that a mesh axis runs over, the one named last changes fastest.
Arguments:
- frames: bfloat16 [2, 32, 42, 64, 192], P('section', 'dp'), may hold values from -4 to 4
- action_ids: int32 [2, 32, 42], P('section', 'dp'), may hold values from 0 to 16
- delta_ids: int32 [2, 32, 42, 4], P('section', 'dp'), may hold values from 0 to 1023
- seq_len: int32 [2, 32], P(None, 'dp'), may hold values from 8 to 21, as said below
- enc_w1: bfloat16 [48, 128], replicated, may hold values from -0.875 to 0.875
- enc_w2: bfloat16 [512, 512], replicated, may hold values from -0.25 to 0.25
- codebook: bfloat16 [1024, 512], replicated, may hold values from -6 to 6
- action_table: bfloat16 [17, 512], replicated, may hold values from -6 to 6
- ln_gain: float32 [2, 512, 2], replicated, may hold values from 0.25 to 1.75
- ln_bias: float32 [2, 512, 2], replicated, may hold values from -2 to 2
- w_qkv: bfloat16 [2, 512, 1536], replicated, may hold values from -0.25 to 0.25
- w_out: bfloat16 [2, 512, 512], replicated, may hold values from -1 to 1
- w_up: bfloat16 [2, 512, 2048], replicated, may hold values from -0.25 to 0.25
- w_down: bfloat16 [2, 2048, 512], replicated, may hold values from -0.125 to 0.125
- cotangent: bfloat16 [2, 32, 252, 512], P('section', 'dp'), may hold values from -6 to 6
Outputs:
- activations: bfloat16 [2, 32, 252, 512], P('section', 'dp')
- embed_grad: bfloat16 [2, 32, 252, 512], P('section', 'dp')
- grad_qkv: float32 [2, 2, 512, 1536], P('section', None, 'dp')
- grad_out: float32 [2, 2, 512, 512], P('section', None, 'dp')
- grad_up: float32 [2, 2, 512, 2048], P('section', None, 'dp')
- grad_down: float32 [2, 2, 2048, 512], P('section', None, 'dp')
- grad_gain: float32 [2, 2, 512, 2], P('section', None, 'dp')
- grad_bias: float32 [2, 2, 512], P('section', None, 'dp')
- grad_bias_two: float32 [2, 2, 512], P('section', None, 'dp')
- grad_enc1: float32 [2, 48, 128], P('section', None, 'dp')
- grad_enc2: float32 [2, 512, 512], P('section', None, 'dp')
- grad_codebook: float32 [2, 1024, 512], P('section', None, 'dp')
- grad_actions: float32 [2, 17, 512], P('section', None, 'dp')
Inputs may be any that keep to these rules, and one draw needn't show every extreme that they name: `seq_len`: each entry is 8 or 21; the 42 steps of a micro-batch form sequences of that many steps one after the other, the last one shorter where it does not divide 42; both values occur in every draw.
All inputs are finite; a program needn't handle non-finite values.
Results may differ from a plain program's by a relative error of at most 0.019.
Values may be sent and summed in bfloat16 or wider, within the bound.
A program may use at most 256 MiB of HBM per device.

v0:
```python
import jax
import jax.numpy as jnp
from jax import lax
from jax.sharding import PartitionSpec as P

HEADS = 8
HEAD_DIM = 64
CODES = 1024
ACTIONS = 17
FRAME = 64
TPS = 6


EPS = 1e-05


def from_partner(array, axis, distance):
    return lax.ppermute(array, axis, [(i, i ^ 1 << distance) for i in range(lax.axis_size(axis))])


def layer_norm(stream, gain, shift):
    row_mean = jnp.mean(stream, axis=-1, keepdims=True)
    center = stream - row_mean
    spread = jnp.mean(center * center, axis=-1, keepdims=True)
    return center * lax.rsqrt(spread + EPS) * gain + shift


def gelu_exact(values):
    return jax.nn.gelu(values, approximate=False)


def plain_dot(operand, partner):
    return jnp.dot(operand, partner, preferred_element_type=jnp.float32)


def contract_rows(operand, partner):
    return lax.dot_general(
        operand, partner, (((0,), (0,)), ((), ())), preferred_element_type=jnp.float32
    )


def times_transposed(operand, partner):
    return lax.dot_general(
        operand, partner, (((1,), (1,)), ((), ())), preferred_element_type=jnp.float32
    )


def on_device(
    frames,
    action_ids,
    delta_ids,
    seq_len,
    enc_w1,
    enc_w2,
    codebook,
    action_table,
    ln_gain,
    ln_bias,
    w_qkv,
    w_out,
    w_up,
    w_down,
    cotangent,
):
    micro_count, step_count = (frames.shape[1], frames.shape[2])
    frame_count = micro_count * step_count
    row_count = step_count * TPS
    model_width = codebook.shape[1]
    channels = enc_w1.shape[1]
    patch_grid = FRAME // 4
    pool_grid = FRAME // 8
    pooled_cells = pool_grid * pool_grid
    patches = (
        frames[0]
        .reshape(frame_count, patch_grid, 4, patch_grid, 12)
        .transpose(0, 1, 3, 2, 4)
        .reshape(-1, 48)
    )
    first_conv = plain_dot(patches, enc_w1)
    hidden, first_back = jax.vjp(gelu_exact, first_conv)
    hidden = hidden.astype(jnp.bfloat16)
    blocks = (
        hidden.reshape(frame_count, pool_grid, 2, pool_grid, 2, channels)
        .transpose(0, 1, 3, 2, 4, 5)
        .reshape(-1, 4 * channels)
    )
    second = plain_dot(blocks, enc_w2)
    activated, second_back = jax.vjp(gelu_exact, second)
    pooled = jnp.mean(activated.reshape(frame_count, pooled_cells, model_width), axis=1)
    action_hot = (
        action_ids[0].reshape(-1, 1) == jnp.arange(ACTIONS, dtype=jnp.int32)[None, :]
    ).astype(jnp.bfloat16)
    code_hot = (delta_ids[0].reshape(-1, 1) == jnp.arange(CODES, dtype=jnp.int32)[None, :]).astype(
        jnp.bfloat16
    )
    action_rows = plain_dot(action_hot, action_table)
    code_rows = plain_dot(code_hot, codebook).reshape(frame_count, TPS - 2, model_width)
    tokens = jnp.concatenate([pooled[:, None], action_rows[:, None], code_rows], axis=1).astype(
        jnp.bfloat16
    )
    outgoing = tokens.reshape(1, micro_count, row_count, model_width)
    arrived = from_partner(outgoing, "section", 0)
    other_half = 1 - lax.axis_index("section")
    lengths = lax.dynamic_index_in_dim(seq_len, other_half, 0, keepdims=False)
    step_of_row = jnp.arange(row_count, dtype=jnp.int32) // TPS
    sequence = step_of_row[None, :] // lengths[:, None]
    allowed = (step_of_row[None, None, :] <= step_of_row[None, :, None]) & (
        sequence[:, :, None] == sequence[:, None, :]
    )
    score_scale = HEAD_DIM ** (-0.5)
    stream = arrived[0].reshape(-1, model_width).astype(jnp.float32)
    layers = w_qkv.shape[0]
    kept_state = []
    for depth in range(layers):
        normed, norm_back = jax.vjp(layer_norm, stream, ln_gain[depth, :, 0], ln_bias[depth, :, 0])
        normed_low = normed.astype(jnp.bfloat16)
        packed = plain_dot(normed_low, w_qkv[depth]).astype(jnp.bfloat16)
        qkv_heads = packed.reshape(micro_count, row_count, 3, HEADS, HEAD_DIM)
        queries, key_rows, values = (qkv_heads[:, :, 0], qkv_heads[:, :, 1], qkv_heads[:, :, 2])
        scores = (
            jnp.einsum("bqhd,bkhd->bhqk", queries, key_rows, preferred_element_type=jnp.float32)
            * score_scale
        )
        scores = jnp.where(allowed[:, None], scores, -jnp.inf)
        row_max = jnp.max(scores, axis=-1, keepdims=True)
        exp_terms = jnp.exp(scores - row_max)
        soft_weights = exp_terms / jnp.sum(exp_terms, axis=-1, keepdims=True)
        soft_low = soft_weights.astype(jnp.bfloat16)
        attended = (
            jnp.einsum("bhqk,bkhd->bqhd", soft_low, values, preferred_element_type=jnp.float32)
            .astype(jnp.bfloat16)
            .reshape(-1, model_width)
        )
        middle = stream + plain_dot(attended, w_out[depth])
        normed_two, norm_two_back = jax.vjp(
            layer_norm, middle, ln_gain[depth, :, 1], ln_bias[depth, :, 1]
        )
        normed_two_low = normed_two.astype(jnp.bfloat16)
        upward = plain_dot(normed_two_low, w_up[depth])
        gated_rows, gelu_back = jax.vjp(gelu_exact, upward)
        gated_low = gated_rows.astype(jnp.bfloat16)
        stream = middle + plain_dot(gated_low, w_down[depth])
        kept_state.append(
            (
                norm_back,
                normed_low,
                queries,
                key_rows,
                values,
                soft_weights,
                soft_low,
                attended,
                norm_two_back,
                normed_two_low,
                gelu_back,
                gated_low,
            )
        )
    activations = stream.astype(jnp.bfloat16).reshape(1, micro_count, row_count, model_width)
    upstream = cotangent[0].reshape(-1, model_width).astype(jnp.float32)
    layer_parts = [None] * layers
    for depth in reversed(range(layers)):
        (
            norm_back,
            normed_low,
            queries,
            key_rows,
            values,
            soft_weights,
            soft_low,
            attended,
            norm_two_back,
            normed_two_low,
            gelu_back,
            gated_low,
        ) = kept_state[depth]
        back_down = upstream.astype(jnp.bfloat16)
        part_down = contract_rows(gated_low, back_down)
        back_gated = times_transposed(back_down, w_down[depth])
        back_up = gelu_back(back_gated)[0].astype(jnp.bfloat16)
        part_up = contract_rows(normed_two_low, back_up)
        back_norm_two, gain_two, shift_two = norm_two_back(times_transposed(back_up, w_up[depth]))
        back_middle = upstream + back_norm_two
        back_branch = back_middle.astype(jnp.bfloat16)
        part_out = contract_rows(attended, back_branch)
        back_attended = (
            times_transposed(back_branch, w_out[depth])
            .astype(jnp.bfloat16)
            .reshape(micro_count, row_count, HEADS, HEAD_DIM)
        )
        back_probs = jnp.einsum(
            "bqhd,bkhd->bhqk", back_attended, values, preferred_element_type=jnp.float32
        )
        back_values = jnp.einsum(
            "bhqk,bqhd->bkhd", soft_low, back_attended, preferred_element_type=jnp.float32
        )
        back_scores = (
            soft_weights * (back_probs - jnp.sum(soft_weights * back_probs, axis=-1, keepdims=True))
        ).astype(jnp.bfloat16)
        back_queries = (
            jnp.einsum("bhqk,bkhd->bqhd", back_scores, key_rows, preferred_element_type=jnp.float32)
            * score_scale
        )
        back_keys = (
            jnp.einsum("bhqk,bqhd->bkhd", back_scores, queries, preferred_element_type=jnp.float32)
            * score_scale
        )
        back_packed = (
            jnp.stack([back_queries, back_keys, back_values], axis=2)
            .astype(jnp.bfloat16)
            .reshape(-1, 3 * model_width)
        )
        part_qkv = contract_rows(normed_low, back_packed)
        back_norm, gain_one, shift_one = norm_back(times_transposed(back_packed, w_qkv[depth]))
        upstream = back_middle + back_norm
        part_gains = jnp.stack([gain_one, gain_two], axis=-1)
        layer_parts[depth] = (
            part_qkv,
            part_out,
            part_up,
            part_down,
            part_gains,
            shift_one,
            shift_two,
        )
    returned = from_partner(
        upstream.astype(jnp.bfloat16).reshape(1, micro_count, row_count, model_width), "section", 0
    )
    back_tokens = returned[0].reshape(frame_count, TPS, model_width)
    part_actions = contract_rows(action_hot, back_tokens[:, 1])
    part_codes = contract_rows(code_hot, back_tokens[:, 2:].reshape(-1, model_width))
    back_pool = jnp.broadcast_to(
        back_tokens[:, 0:1].astype(jnp.float32) / pooled_cells,
        (frame_count, pooled_cells, model_width),
    ).reshape(-1, model_width)
    back_second = second_back(back_pool)[0].astype(jnp.bfloat16)
    part_second = contract_rows(blocks, back_second)
    back_blocks = times_transposed(back_second, enc_w2)
    back_hidden = (
        back_blocks.reshape(frame_count, pool_grid, pool_grid, 2, 2, channels)
        .transpose(0, 1, 3, 2, 4, 5)
        .reshape(-1, channels)
    )
    back_first = first_back(back_hidden)[0].astype(jnp.bfloat16)
    part_first = contract_rows(patches, back_first)
    local_qkv, local_out, local_up, local_down, local_gain, local_bias, local_bias_two = [
        jnp.stack([layer_parts[depth][member] for depth in range(layers)], axis=0)[None]
        for member in range(7)
    ]
    summed = (
        lax.psum_scatter(local_qkv, "dp", scatter_dimension=2, tiled=True),
        lax.psum_scatter(local_out, "dp", scatter_dimension=2, tiled=True),
        lax.psum_scatter(local_up, "dp", scatter_dimension=2, tiled=True),
        lax.psum_scatter(local_down, "dp", scatter_dimension=2, tiled=True),
        lax.psum_scatter(local_gain, "dp", scatter_dimension=2, tiled=True),
        lax.psum_scatter(local_bias, "dp", scatter_dimension=2, tiled=True),
        lax.psum_scatter(local_bias_two, "dp", scatter_dimension=2, tiled=True),
        lax.psum_scatter(part_first[None], "dp", scatter_dimension=2, tiled=True),
        lax.psum_scatter(part_second[None], "dp", scatter_dimension=2, tiled=True),
        lax.psum_scatter(part_codes[None], "dp", scatter_dimension=2, tiled=True),
        lax.psum_scatter(part_actions[None], "dp", scatter_dimension=2, tiled=True),
    )
    (
        grad_qkv,
        grad_out,
        grad_up,
        grad_down,
        grad_gain,
        grad_bias,
        grad_bias_two,
        grad_enc1,
        grad_enc2,
        grad_codebook,
        grad_actions,
    ) = summed
    return (
        activations,
        returned,
        grad_qkv,
        grad_out,
        grad_up,
        grad_down,
        grad_gain,
        grad_bias,
        grad_bias_two,
        grad_enc1,
        grad_enc2,
        grad_codebook,
        grad_actions,
    )


def solution(mesh):
    return jax.shard_map(
        on_device,
        mesh=mesh,
        in_specs=(
            P("section", "dp", None, None, None),
            P("section", "dp", None),
            P("section", "dp", None, None),
            P(None, "dp"),
            P(),
            P(),
            P(),
            P(),
            P(),
            P(),
            P(),
            P(),
            P(),
            P(),
            P("section", "dp", None, None),
        ),
        out_specs=(
            P("section", "dp", None, None),
            P("section", "dp", None, None),
            P("section", None, "dp", None),
            P("section", None, "dp", None),
            P("section", None, "dp", None),
            P("section", None, "dp", None),
            P("section", None, "dp", None),
            P("section", None, "dp"),
            P("section", None, "dp"),
            P("section", None, "dp"),
            P("section", None, "dp"),
            P("section", None, "dp"),
            P("section", None, "dp"),
        ),
        check_vma=False,
    )
```

profile of v0, /device:TPU:0, one launch (start us, length us, event | category | flops | bytes accessed | tf_op | source)
XLA Modules:
  0.0 1039.1 jit_solution(16960182737417000555)
XLA Ops:
  7.2 13.7 %copy.135 = bf16[1,2,42,64,192]{2,1,3,4,0:T(2,128)(2,1)} copy(bf16[1,2,42,64,192]{4,3,2,1,0:T(8,128)(2,1)} %param.15) | data formatting | bytes 4128768 | tf_op args[0]
  21.0 11.9 %reshape_squeeze.12 = bf16[84,16,4,16,12]{0,2,1,4,3:T(4,128)(2,1)} reshape(bf16[1,2,42,64,192]{2,1,3,4,0:T(2,128)(2,1)} %copy.135) | data formatting | bytes 4128768 | tf_op jit(solution)/shard_map/reshape;squeeze | solution.py:75
  32.9 21.5 %copy.136 = bf16[84,16,16,4,12]{2,1,0,4,3:T(8,128)(2,1)} copy(bf16[84,16,16,4,12]{0,3,1,4,2:T(4,128)(2,1)} %bitcast.314) | data formatting | bytes 4128768 | tf_op jit(solution)/shard_map/transpose | solution.py:76
  54.4 32.9 %reshape.598 = bf16[21504,48]{0,1:T(8,128)(2,1)} reshape(bf16[84,16,16,4,12]{2,1,0,4,3:T(8,128)(2,1)} %copy.136) | data formatting | bytes 4128768 | tf_op jit(solution)/shard_map/reshape | solution.py:77
  87.3 27.7 %multiply_convert_fusion = (bf16[21504,128]{1,0:T(8,128)(2,1)S(1)}, f32[21504,128]{1,0:T(8,128)}, f32[21504,128]{1,0:T(8,128)}) fusion(bf16[21504,48]{0,1:T(8,128)(2,1)} %reshape.598, bf16[48,128]{1,0:T(8,128)(2,1)S(1)} %copy-done.64), kind=kOutput, calls=%fused_computation.28 | convolution fusion | flops 443154432 | bytes 29601792 | tf_op jit(solution)/shard_map/dot_general | solution.py:33
  117.0 27.6 %multiply_multiply_fusion.10 = (f32[5376,512]{1,0:T(8,128)}, f32[5376,512]{1,0:T(8,128)}, f32[5376,512]{1,0:T(8,128)}) fusion(bf16[5376,512]{1,0:T(8,128)(2,1)S(1)} %bitcast.317, bf16[512,512]{1,0:T(8,128)(2,1)S(1)} %copy-done.34), kind=kOutput, calls=%fused_computation.43 | convolution fusion | flops 2994733056 | bytes 39059456 | tf_op jit(solution)/shard_map/dot_general | solution.py:33
  144.6 6.0 reduce_sum.253
  152.9 3.0 collective-permute-start
  157.5 10.3 collective-permute-done
  169.3 3.7 convolution_convert_fusion.1
  173.1 5.0 reshape.631
  178.0 3.3 fusion.165
  194.4 13.1 %multiply_convert_fusion.4 = (bf16[504,2048]{1,0:T(8,128)(2,1)S(1)}, f32[504,2048]{1,0:T(8,128)}, f32[504,2048]{1,0:T(8,128)}) fusion(bf16[2,512,2048]{2,1,0:T(8,128)(2,1)} %param.27, f32[504,512]{1,0:T(8,128)S(1)} %get-tuple-element.118, f32[512]{0:T(512)S(1)} %bitcast.335, f32[512]{0:T(512)S(1)} %bitcast.329, f32[504]{0:T(512)S(1)} %fusion.143, ...), kind=kOutput, calls=%fused_computation.75 | convolution fusion | flops 1125347328 | bytes 13459392 | tf_op jit(solution)/shard_map/dot_general | solution.py:33
  212.8 5.1 reshape.632
  217.9 3.5 fusion.164
  227.7 3.2 fusion.171
  239.9 12.8 %multiply_convert_fusion.3 = (bf16[504,2048]{1,0:T(8,128)(2,1)}, f32[504,2048]{1,0:T(8,128)S(1)}, f32[504,2048]{1,0:T(8,128)S(1)}) fusion(bf16[2,512,2048]{2,1,0:T(8,128)(2,1)} %param.27, f32[504,512]{1,0:T(8,128)S(1)} %get-tuple-element.125, f32[512]{0:T(512)S(1)} %bitcast.333, f32[512]{0:T(512)S(1)} %bitcast.325, f32[504]{0:T(512)S(1)} %fusion.145, ...), kind=kOutput, calls=%fused_computation.62 | convolution fusion | flops 1125347328 | bytes 13459392 | tf_op jit(solution)/shard_map/dot_general | solution.py:33
  265.8 3.5 multiply_reduce_fusion.1
  273.1 2.8 copy.160
  275.9 3.7 convert_element_type.176
  279.6 3.3 multiply_reduce_fusion.4
  297.8 3.5 multiply_reduce_fusion
  308.9 2.8 copy.167
  311.7 3.8 convert_element_type.182
  315.5 3.6 multiply_reduce_fusion.6
  329.4 6.6 collective-permute-done.1
  340.6 9.7 fusion.9
  350.3 8.6 convolution_bitcast_fusion.8
  362.1 3.2 convolution_bitcast_fusion.6
  365.3 3.7 copy.170
  368.9 6.1 copy.171
  383.9 3.1 maximum_bitcast_fusion.2
  388.1 3.0 convolution_bitcast_fusion
  392.4 4.2 maximum_bitcast_fusion.1
  397.2 3.2 convolution_bitcast_fusion.3
  402.0 3.9 maximum_bitcast_fusion
  408.4 3.5 fusion.91
  414.7 24.1 %reduce-scatter.27.cloned.1.call-done = f32[32,2]{1,0:T(8,128)} async-done(((f32[512,2]{1,0:T(8,128)}), f32[32,2]{1,0:T(8,128)}) %reduce-scatter.27.cloned.1.call-update) | async-done | bytes 272
  440.1 56.5 %reduce-scatter.25.cloned.1.call-done = f32[32,4]{1,0:T(8,128)} async-done(((f32[512,4]{1,0:T(8,128)}), f32[32,4]{1,0:T(8,128)}) %reduce-scatter.25.cloned.1.call-update) | async-done | bytes 528
  498.1 5.2 fusion.173
  503.4 6.9 copy.168
  510.3 10.2 fusion.101
  522.9 58.2 %all-reduce = f32[1,48,128]{1,0,2:T(1,128)S(1)} all-reduce(f32[1,48,128]{1,0,2:T(1,128)S(1)} %copy.169), channel_id=9, replica_groups=mesh['section'=2,'dp'=16] {'dp'}, use_global_device_ids=true, to_apply=%region_38.39.clone | all-reduce | flops 6144 | bytes 49152
  583.1 77.7 %all-reduce.6.cloned.1.call-done = (f32[1,512,512]{1,0,2:T(1,128)}, f32[1,1024,512]{1,0,2:T(1,128)}) async-done(((f32[1,512,512]{1,0,2:T(1,128)}, f32[1,1024,512]{1,0,2:T(1,128)}), (f32[1,512,512]{1,0,2:T(1,128)}, f32[1,1024,512]{1,0,2:T(1,128)})) %all-reduce.6.cloned.1.call-update) | async-done | bytes 3145744
  663.9 61.3 %reduce-scatter.19.cloned.1.call-done = f32[1,2,32,512]{3,2,1,0:T(8,128)} async-done(((f32[1,2,512,512]{3,2,1,0:T(8,128)}), f32[1,2,32,512]{3,2,1,0:T(8,128)}) %reduce-scatter.19.cloned.1.call-update) | async-done | bytes 131088 | tf_op jit(solution)/shard_map/reduce_scatter | solution.py:252
  725.2 89.3 %reduce-scatter.17.cloned.1.call-done = f32[1,2,32,1536]{3,2,1,0:T(8,128)} async-done(((f32[1,2,512,1536]{3,2,1,0:T(8,128)}), f32[1,2,32,1536]{3,2,1,0:T(8,128)}) %reduce-scatter.17.cloned.1.call-update) | async-done | bytes 393232 | tf_op jit(solution)/shard_map/reduce_scatter | solution.py:251
  814.5 108.4 %reduce-scatter.23.cloned.1.call-done = f32[1,2,128,512]{3,2,1,0:T(8,128)} async-done(((f32[1,2,2048,512]{3,2,1,0:T(8,128)}), f32[1,2,128,512]{3,2,1,0:T(8,128)}) %reduce-scatter.23.cloned.1.call-update) | async-done | bytes 524304 | tf_op jit(solution)/shard_map/reduce_scatter | solution.py:254
  922.9 109.2 %reduce-scatter.21.cloned.1.call-done = f32[1,2,32,2048]{3,2,1,0:T(8,128)} async-done(((f32[1,2,512,2048]{3,2,1,0:T(8,128)}), f32[1,2,32,2048]{3,2,1,0:T(8,128)}) %reduce-scatter.21.cloned.1.call-update) | async-done | bytes 524304 | tf_op jit(solution)/shard_map/reduce_scatter | solution.py:253
  (297 shorter events, 125.1 us)
Async XLA Ops:
  7.2 143.9 %copy-start = (bf16[1024,512]{1,0:T(8,128)(2,1)S(1)}, bf16[1024,512]{1,0:T(8,128)(2,1)}, u32[]{:S(2)}) copy-start(bf16[1024,512]{1,0:T(8,128)(2,1)} %param.21) | copy-start | bytes 3145732
  7.2 406.2 %reduce-scatter.29.cloned.1.call-start = ((), (), s32[]{:S(2)}) async-start(), calls=%async_computation.14 | async-start | bytes 278528
  54.4 32.9 %copy-start.64 = (bf16[48,128]{1,0:T(8,128)(2,1)S(1)}, bf16[48,128]{1,0:T(8,128)(2,1)}, u32[]{:S(2)}) copy-start(bf16[48,128]{1,0:T(8,128)(2,1)} %param.19) | copy-start | bytes 36868
  117.0 27.6 %copy-start.10 = (bf16[84,8,2,8,2,128]{5,3,4,2,1,0:T(8,128)(2,1)}, bf16[84,8,2,8,2,128]{5,3,4,2,1,0:T(8,128)(2,1)S(1)}, u32[]{:S(2)}) copy-start(bf16[84,8,2,8,2,128]{5,3,4,2,1,0:T(8,128)(2,1)S(1)} %copy.137) | copy-start | bytes 16515076
  144.6 6.2 copy-start.54
  144.6 7.1 copy-start.65
  144.6 7.2 copy-start.46
  150.6 5.4 copy-start.50
  150.6 5.4 copy-start.51
  150.6 5.4 copy-start.57
  150.6 5.7 copy-start.40
  151.0 5.3 copy-start.52
  151.8 4.3 copy-start.55
  152.9 15.0 %collective-permute-start = (bf16[1,2,252,512]{3,2,1,0:T(8,128)(2,1)S(1)}, bf16[1,2,252,512]{3,2,1,0:T(8,128)(2,1)S(1)}, u32[]{:S(2)}, u32[]{:S(2)}) collective-permute-start(bf16[1,2,252,512]{3,2,1,0:T(8,128)(2,1)S(1)} %convert_element_type.150), channel_id=1, source_target_pairs={{0,16},{16,0},{1,17},{17,1},{2,18},{18,2},{3,19},{19,3},{4,20},{20... | collective-permute-start | bytes 1548296 | tf_op jit(solution)/shard_map/ppermute | solution.py:18
  156.0 17.1 %copy-start.47 = (f32[1,512,1]{1,2,0:T(1,128)}, f32[1,512,1]{1,2,0:T(1,128)S(1)}, u32[]{:S(2)}) copy-start(f32[1,512,1]{1,2,0:T(1,128)S(1)} %get-tuple-element.105) | copy-start | bytes 6148
  156.0 38.3 %copy-start.42 = (f32[1,512,1]{1,2,0:T(1,128)}, f32[1,512,1]{1,2,0:T(1,128)S(1)}, u32[]{:S(2)}) copy-start(f32[1,512,1]{1,2,0:T(1,128)S(1)} %get-tuple-element.108) | copy-start | bytes 6148
  168.0 10.0 copy-start.44
  169.3 8.7 copy-start.41
  183.1 4.1 copy-start.11
  185.0 4.1 copy-start.13
  192.0 15.5 %copy-start.18 = (bf16[504,512]{0,1:T(8,128)(2,1)}, bf16[504,512]{0,1:T(8,128)(2,1)S(1)}, u32[]{:S(2)}) copy-start(bf16[504,512]{0,1:T(8,128)(2,1)S(1)} %reshape.604) | copy-start | bytes 1548292
  192.1 15.4 %copy-start.5 = (f32[504,512]{1,0:T(8,128)}, f32[504,512]{1,0:T(8,128)S(1)}, u32[]{:S(2)}) copy-start(f32[504,512]{1,0:T(8,128)S(1)} %reshape.619) | copy-start | bytes 3096580
  194.4 13.2 %copy-start.60 = (bf16[2,2048,512]{2,1,0:T(8,128)(2,1)S(1)}, bf16[2,2048,512]{2,1,0:T(8,128)(2,1)}, u32[]{:S(2)}) copy-start(bf16[2,2048,512]{2,1,0:T(8,128)(2,1)} %param.28) | copy-start | bytes 12582916
  208.9 74.0 %copy-start.3 = (f32[504,512]{1,0:T(8,128)}, f32[504,512]{1,0:T(8,128)S(1)}, u32[]{:S(2)}) copy-start(f32[504,512]{1,0:T(8,128)S(1)} %get-tuple-element.121) | copy-start | bytes 3096580
  223.2 7.8 copy-start.15
  239.9 12.8 %copy-start.19 = (bf16[504,512]{1,0:T(8,128)(2,1)S(1)}, bf16[504,512]{1,0:T(8,128)(2,1)}, u32[]{:S(2)}) copy-start(bf16[504,512]{1,0:T(8,128)(2,1)} %reshape_squeeze.13) | copy-start | bytes 1548292
  239.9 12.8 %copy-start.61 = (bf16[2,2048,512]{2,1,0:T(8,128)(2,1)S(1)}, bf16[2,2048,512]{2,1,0:T(8,128)(2,1)}, u32[]{:S(2)}) copy-start(bf16[2,2048,512]{2,1,0:T(8,128)(2,1)} %param.28) | copy-start | bytes 12582916
  279.6 4.1 copy-start.69
  279.6 4.8 copy-start.70
  283.6 7.0 copy-start.25
  307.1 8.3 copy-start.49
  307.1 8.4 copy-start.48
  322.5 13.4 %collective-permute-start.1 = (bf16[1,2,252,512]{3,2,1,0:T(8,128)(2,1)}, bf16[1,2,252,512]{3,2,1,0:T(8,128)(2,1)}, u32[]{:S(2)}, u32[]{:S(2)}) collective-permute-start(bf16[1,2,252,512]{3,2,1,0:T(8,128)(2,1)} %reshape.610), channel_id=1, source_target_pairs={{0,16},{16,0},{1,17},{17,1},{2,18},{18,2},{3,19},{19,3},{4,20},{20... | collective-permute-start | bytes 1548296 | tf_op jit(solution)/shard_map/ppermute | solution.py:18
  325.2 113.6 %reduce-scatter.27.cloned.1.call-start = ((), (), s32[]{:S(2)}) async-start(), calls=%async_computation.13 | async-start | bytes 278528
  326.1 170.5 %reduce-scatter.25.cloned.1.call-start = ((), (), s32[]{:S(2)}) async-start(), calls=%async_computation.12 | async-start | bytes 278528
  329.3 252.4 %reduce-scatter.31.cloned.1.call-start = ((), (), s32[]{:S(2)}) async-start(), calls=%async_computation.15 | async-start | bytes 278528
  350.3 8.6 copy-start.2
  350.3 8.6 copy-start.56
  350.3 11.8 %copy-start.53 = (s32[336]{0:T(512)S(1)}, s32[336]{0:T(512)}, u32[]{:S(2)}) copy-start(s32[336]{0:T(512)} %copy-done.52) | copy-start | bytes 4036
  362.0 298.8 %all-reduce.6.cloned.1.call-start = ((), (), s32[]{:S(2)}) async-start(), calls=%async_computation.16 | async-start | bytes 6291456
  375.1 350.1 %reduce-scatter.19.cloned.1.call-start = ((), (), s32[]{:S(2)}) async-start(), calls=%async_computation.9 | async-start | bytes 2228224 | tf_op jit(solution)/shard_map/reduce_scatter | solution.py:252
  379.8 434.7 %reduce-scatter.17.cloned.1.call-start = ((), (), s32[]{:S(2)}) async-start(), calls=%async_computation.8 | async-start | bytes 6684672 | tf_op jit(solution)/shard_map/reduce_scatter | solution.py:251
  387.1 535.9 %reduce-scatter.23.cloned.1.call-start = ((), (), s32[]{:S(2)}) async-start(), calls=%async_computation.11 | async-start | bytes 8912896 | tf_op jit(solution)/shard_map/reduce_scatter | solution.py:254
  387.1 3.9 copy-start.26
  396.6 635.5 %reduce-scatter.21.cloned.1.call-start = ((), (), s32[]{:S(2)}) async-start(), calls=%async_computation.10 | async-start | bytes 8912896 | tf_op jit(solution)/shard_map/reduce_scatter | solution.py:253
  408.4 89.7 %copy-start.35 = (bf16[512,512]{1,0:T(8,128)(2,1)S(1)}, bf16[512,512]{1,0:T(8,128)(2,1)}, u32[]{:S(2)}) copy-start(bf16[512,512]{1,0:T(8,128)(2,1)} %param.20) | copy-start | bytes 1572868
  503.4 6.9 copy-start.29
  510.3 521.8 %copy-start.1 = (bf16[1024,512]{1,0:T(8,128)(2,1)S(1)}, bf16[1024,512]{1,0:T(8,128)(2,1)}, u32[]{:S(2)}) copy-start(bf16[1024,512]{1,0:T(8,128)(2,1)} %param.21) | copy-start | bytes 3145732
  (34 other events, 73.6 us)
Sparse Core Ops, SparseCore 0:
  325.3 55.5 reduce-scatter.28
  384.4 54.2 reduce-scatter.26
  442.3 54.2 reduce-scatter.24
  500.0 54.3 reduce-scatter.30
  557.9 102.8 all-reduce.5
  665.0 60.1 reduce-scatter.18
  730.2 84.2 reduce-scatter.16
  819.1 103.7 reduce-scatter.22
  927.6 104.4 reduce-scatter.20
where the time goes:
time: 1050 us; the launch traced here: 1040 us
  waiting for transfers between devices  543 us (52%)
  local copies, waits for them, and re-layouts  192 us (18%)
  matrix products  177 us (17%)
  blocking collectives  58.2 us (6%)
  other arithmetic  45.3 us (4%)
  between operations  16.8 us (2%)
    unnamed x14, waiting for transfers between devices  158 us
    reduce_scatter x1, waiting for transfers between devices, on_device(): lax.psum_scatter(local_up, 'dp', scatter_dimension=2, tiled=True)  109 us
    reduce_scatter x1, waiting for transfers between devices, on_device(): lax.psum_scatter(local_down, 'dp', scatter_dimension=2, tiled=True)  108 us
    dot_general x12, matrix products, plain_dot(): return jnp.dot(operand, partner, preferred_element_type=jnp.float32)  96.5 us
    reduce_scatter x1, waiting for transfers between devices, on_device(): lax.psum_scatter(local_qkv, 'dp', scatter_dimension=2, tiled=True)  89.3 us
    reduce_scatter x1, waiting for transfers between devices, on_device(): lax.psum_scatter(local_out, 'dp', scatter_dimension=2, tiled=True)  61.3 us
    unnamed x1, blocking collectives  58.2 us
    unnamed x169, local copies, waits for them, and re-layouts  55 us
  transfers between devices with their start and end apart: 11, of which 9 were waited for; matrix products, arithmetic and copies ran while one was open for 11% of the time, Pallas kernels for 0%

commit v1 on v0

v1 whole, which is shorter than its diff:
```python
import functools

import jax
import jax.numpy as jnp
from jax import lax
from jax.experimental import pallas as pl
from jax.experimental.pallas import tpu as pltpu
from jax.sharding import PartitionSpec as P

HEADS = 8
HEAD_DIM = 64
TPS = 6
EPS = 1e-05
BF = jnp.bfloat16
F32 = jnp.float32
I32 = jnp.int32

WIDTH = 512
CODES = 1024
FRAMES_BLOCK = 28
BLOCK_ROWS = FRAMES_BLOCK * 8
TABLE = 1152
POOL_AT = 1056
ACT_AT = 1024
LAYER_COLS = 6144
ENC_COLS = 1664
VMEM_LIMIT = 60 << 20


def dot(a, b):
    return jnp.dot(a, b, preferred_element_type=F32)


def dot_rows(a, b):
    return lax.dot_general(a, b, (((0,), (0,)), ((), ())), preferred_element_type=F32)


def dot_lanes(a, b):
    return lax.dot_general(a, b, (((1,), (1,)), ((), ())), preferred_element_type=F32)


def iota(shape, axis):
    return lax.broadcasted_iota(I32, shape, axis)


def gelu_pair(v):
    e = jnp.exp2(v * v * (-0.5 * 1.4426950408889634))
    t = 1.0 / (1.0 + 0.23164190 * jnp.abs(v))
    poly = 0.5 * 1.061405429
    poly = poly * t + 0.5 * -1.453152027
    poly = poly * t + 0.5 * 1.421413741
    poly = poly * t + 0.5 * -0.284496736
    poly = poly * t + 0.5 * 0.254829592
    tail = poly * t * e
    cdf = jnp.where(v >= 0, 1.0 - tail, tail)
    return v * cdf, cdf + v * e * 0.3989422804014327


def patch_index(rows):
    k = iota((rows, 48), 0)
    dy = (k * 2731) >> 16
    rest = k - dy * 24
    j = jnp.where(rest >= 12, rest - 12, rest)
    return jnp.where((iota((rows, 48), 1) == dy * 12 + j) & (k < 96), 1.0, 0.0), rest


def encoder_weights(w1):
    hot, rest = patch_index(128)
    wide = dot(hot.astype(BF), w1)
    first = jnp.where(rest[:, :1] < 12, wide, 0.0)
    second = jnp.where(rest[:, :1] >= 12, wide, 0.0)
    block = jnp.concatenate([first, second], axis=1)
    zero = jnp.zeros_like(block)
    return jnp.concatenate(
        [jnp.concatenate([block, zero], axis=1), jnp.concatenate([zero, block], axis=1)], axis=0
    ).astype(BF)


def enc_fwd_kernel(
    frames, w1, w2, book, acts, ids, tok, xl, blocks, g1, g2, perm, lanes, big, xs, acc, table
):
    step = pl.program_id(0)

    @pl.when(step == 0)
    def _():
        a, b = iota((256, 256), 0), iota((256, 256), 1)
        perm[...] = jnp.where(b == 8 * (a & 31) + (a >> 5), 1.0, 0.0).astype(BF)
        src = iota((192, 1024), 0)
        px = (src * 5462) >> 16
        at = (px >> 1) * 128 + (px & 1) * 12 + (src - px * 12)
        out = iota((192, 1024), 1)
        for dy in range(4):
            lanes[dy] = jnp.where(out == at + dy * 24, 1.0, 0.0).astype(BF)
        big[...] = encoder_weights(w1[...])
        table[pl.ds(0, CODES), :] = book[...]
        named = acts[...].astype(F32)
        pad = jnp.zeros((TABLE - ACT_AT - named.shape[0], WIDTH), F32)
        table[pl.ds(ACT_AT, TABLE - ACT_AT), :] = jnp.concatenate([named, pad], axis=0).astype(BF)

    for group in range(FRAMES_BLOCK // 4):
        rows = frames[pl.ds(group * 4, 4)].reshape(256, 192)
        moved = dot(perm[...], rows).astype(BF).reshape(8, 32, 192)
        xs[:, pl.ds(group * 32, 32), :] = moved
    for dy2 in range(2):
        spread = dot(xs[dy2 * 4], lanes[0])
        for dy in range(1, 4):
            spread += dot(xs[dy2 * 4 + dy], lanes[dy])
        spread = spread.astype(BF)
        for bx in range(8):
            xl[0, pl.ds(bx * BLOCK_ROWS, BLOCK_ROWS), pl.ds(dy2 * 128, 128)] = spread[
                :, bx * 128 : (bx + 1) * 128
            ]
    acc[...] = jnp.zeros_like(acc)

    def part(bx, _):
        rows = pl.ds(pl.multiple_of(bx * BLOCK_ROWS, BLOCK_ROWS), BLOCK_ROWS)
        value, slope = gelu_pair(dot(xl[0, rows, :], big[...]))
        value = value.astype(BF)
        blocks[0, rows, :] = value
        g1[0, rows, :] = slope.astype(BF)
        value, slope = gelu_pair(dot(value, w2[...]))
        g2[0, rows, :] = slope.astype(BF)
        acc[...] += value
        return 0

    lax.fori_loop(0, 8, part, 0)
    pooled = jnp.sum(acc[...].reshape(FRAMES_BLOCK, 8, WIDTH), axis=1) * (1.0 / 64.0)
    pooled = jnp.concatenate([pooled, jnp.zeros((32 - FRAMES_BLOCK, WIDTH), F32)], axis=0)
    table[pl.ds(pl.multiple_of(POOL_AT + step * 32, 32), 32), :] = pooled.astype(BF)

    @pl.when(step == pl.num_programs(0) - 1)
    def _():
        for part_at in range(2):
            rows = pl.ds(part_at * 256, 256)
            hot = jnp.where(iota((256, TABLE), 1) == ids[rows, :], 1.0, 0.0).astype(BF)
            tok[rows, :] = dot(hot, table[...]).astype(BF)


def enc_forward(frames, w1, w2, book, acts, ids):
    count = frames.shape[0]
    grid = count // FRAMES_BLOCK
    rows = 8 * BLOCK_ROWS

    def whole(shape):
        return pl.BlockSpec(shape, lambda i: (0,) * len(shape))

    def saved(lanes):
        return pl.BlockSpec((1, rows, lanes), lambda i: (i, 0, 0))

    return pl.pallas_call(
        enc_fwd_kernel,
        grid=(grid,),
        in_specs=[
            pl.BlockSpec((FRAMES_BLOCK, 64, 192), lambda i: (i, 0, 0)),
            whole(w1.shape),
            whole(w2.shape),
            whole(book.shape),
            whole(acts.shape),
            whole(ids.shape),
        ],
        out_specs=[whole((512, WIDTH)), saved(256), saved(512), saved(512), saved(512)],
        out_shape=[
            jax.ShapeDtypeStruct((512, WIDTH), BF),
            jax.ShapeDtypeStruct((grid, rows, 256), BF),
            jax.ShapeDtypeStruct((grid, rows, 512), BF),
            jax.ShapeDtypeStruct((grid, rows, 512), BF),
            jax.ShapeDtypeStruct((grid, rows, 512), BF),
        ],
        scratch_shapes=[
            pltpu.VMEM((256, 256), BF),
            pltpu.VMEM((4, 192, 1024), BF),
            pltpu.VMEM((256, 512), BF),
            pltpu.VMEM((8, BLOCK_ROWS, 192), BF),
            pltpu.VMEM((BLOCK_ROWS, WIDTH), F32),
            pltpu.VMEM((TABLE, WIDTH), BF),
        ],
        compiler_params=pltpu.CompilerParams(vmem_limit_bytes=VMEM_LIMIT),
        name="enc_fwd",
    )(frames, w1, w2, book, acts, ids)


def ln_parts(x):
    mean = jnp.mean(x, axis=-1, keepdims=True)
    center = x - mean
    var = jnp.mean(center * center, axis=-1, keepdims=True)
    scale = lax.rsqrt(var + EPS)
    return center * scale, scale


def ln_back(x, d, gain):
    hat, scale = ln_parts(x)
    dh = d * gain
    one = jnp.mean(dh, axis=-1, keepdims=True)
    two = jnp.mean(dh * hat, axis=-1, keepdims=True)
    back = scale * (dh - one - hat * two)
    return back, jnp.sum(d * hat, axis=0, keepdims=True), jnp.sum(d, axis=0, keepdims=True)


def head_mask(h):
    lane = iota((1, 256), 1) >> 6
    return lane == h


def stacked(rows, scale):
    out = []
    for h in range(4):
        mask = jnp.where(head_mask(h), scale, 0.0).astype(BF)
        out.append(rows * mask)
    return jnp.concatenate(out, axis=0)


def unstacked(rows):
    out = rows[768:]
    for h in range(3):
        out = jnp.where(head_mask(h), rows[h * 256 : (h + 1) * 256], out)
    return out


def scatter_rows(g, d, cols, value, dests=16):
    shaped = value.astype(BF).reshape(dests // 2, 2, 32, value.shape[1])
    for core in range(2):
        g[d, core, :, :, cols] = shaped[:, core]


def layers_kernel(
    tok, cot, lens, lnp, wq_h, wo_h, wu_h, wd_h,
    act, eg, g, gl,
    wq, wo, wu, wd, stream, normed, packed, probs, att, normed2, gated, slope, bias,
    up, back_up, back_att, back_packed, lng, sems,
):
    layers = wq.shape[0]
    section = lax.axis_index("section")
    copies = []
    for d in range(layers):
        for k, (src, dst) in enumerate(((wq_h, wq), (wo_h, wo), (wu_h, wu), (wd_h, wd))):
            copy = pltpu.make_async_copy(src.at[d], dst.at[d], sems.at[d, k])
            copy.start()
            copies.append(copy)

    stream[0, 0] = tok[...].astype(F32)
    row = iota((256, 1), 0)
    col = iota((1, 256), 1)
    q_step = ((row * 10923) >> 16).astype(F32)
    k_step = ((col * 10923) >> 16).astype(F32)
    for s in range(2):
        inv = 1.0 / lens[section, s].astype(F32)
        q_seq = jnp.floor((q_step + 0.5) * inv)
        k_seq = jnp.floor((k_step + 0.5) * inv)
        bias[s] = jnp.where((k_step <= q_step) & (q_seq == k_seq), 0.0, -1e30)
    for copy in copies:
        copy.wait()

    def forward(d, _):
        x = stream[d, 0]
        hat, _ = ln_parts(x)
        normed[d] = (hat * lnp[d, 0:1] + lnp[d, 2:3]).astype(BF)
        for c in range(3):
            cols = pl.ds(c * 512, 512)
            packed[d, :, cols] = dot(normed[d], wq[d, :, cols]).astype(BF)
        for s in range(2):
            rows = pl.ds(s * 256, 256)
            for quad in range(2):
                q = stacked(packed[d, rows, pl.ds(quad * 256, 256)], HEAD_DIM**-0.5)
                k = packed[d, rows, pl.ds(512 + quad * 256, 256)]
                v = packed[d, rows, pl.ds(1024 + quad * 256, 256)]
                scores = dot_lanes(q, k).reshape(4, 256, 256) + bias[s][None]
                top = jnp.max(scores, axis=-1, keepdims=True)
                e = jnp.exp(scores - top)
                total = jnp.sum(e, axis=-1, keepdims=True)
                p = (e * (1.0 / total)).astype(BF).reshape(1024, 256)
                probs[d, s * 2 + quad] = p
                att[d, rows, pl.ds(quad * 256, 256)] = unstacked(dot(p, v)).astype(BF)
        middle = stream[d, 0] + dot(att[d], wo[d])
        stream[d, 1] = middle
        hat, _ = ln_parts(middle)
        normed2[d] = (hat * lnp[d, 1:2] + lnp[d, 3:4]).astype(BF)

        def chunk(c, _):
            cols = pl.ds(pl.multiple_of(c * 512, 512), 512)
            value, grad = gelu_pair(dot(normed2[d], wu[d, :, cols]))
            gated[d, :, cols] = value.astype(BF)
            slope[d, :, cols] = grad.astype(BF)
            return 0

        lax.fori_loop(0, 4, chunk, 0)
        stream[d + 1, 0] = stream[d, 1] + dot(gated[d], wd[d])
        return 0

    lax.fori_loop(0, layers, forward, 0)
    for s in range(2):
        act[s] = stream[layers, 0, pl.ds(s * 256, 252), :].astype(BF)
        up[pl.ds(s * 256, 252), :] = cot[s].astype(F32)
        up[pl.ds(s * 256 + 252, 4), :] = jnp.zeros((4, WIDTH), F32)
    lng[...] = jnp.zeros_like(lng)

    def backward(i, _):
        d = layers - 1 - i
        down = up[...].astype(BF)

        def chunk(c, _):
            cols = pl.ds(pl.multiple_of(c * 256, 256), 256)
            part = dot_rows(gated[d, :, cols], down).astype(BF).reshape(2, 4, 32, WIDTH)
            for core in range(2):
                for j in range(4):
                    g[d, core, c, :, pl.ds(4096 + 512 * j, 512)] = part[core, j]
            back = dot_lanes(down, wd[d, cols, :])
            back = (back * slope[d, :, cols].astype(F32)).astype(BF)
            back_up[:, cols] = back
            part = dot_rows(normed2[d], back).astype(BF).reshape(8, 2, 32, 256)
            out = pl.ds(pl.multiple_of(2048 + c * 256, 256), 256)
            for core in range(2):
                g[d, core, :, :, out] = part[:, core]
            return 0

        lax.fori_loop(0, 8, chunk, 0)
        back, gain, shift = ln_back(stream[d, 1], dot_lanes(back_up[...], wu[d]), lnp[d, 1:2])
        lng[pl.ds(d * 4 + 1, 1), :] = gain
        lng[pl.ds(d * 4 + 3, 1), :] = shift
        up[...] += back
        branch = up[...].astype(BF)
        scatter_rows(g, d, pl.ds(1536, 512), dot_rows(att[d], branch))
        back_att[...] = dot_lanes(branch, wo[d]).astype(BF)
        for s in range(2):
            rows = pl.ds(s * 256, 256)
            for quad in range(2):
                lanes = pl.ds(quad * 256, 256)
                qs = stacked(packed[d, rows, lanes], HEAD_DIM**-0.5)
                k = packed[d, rows, pl.ds(512 + quad * 256, 256)]
                v = packed[d, rows, pl.ds(1024 + quad * 256, 256)]
                outs = stacked(back_att[rows, lanes], 1.0)
                p = probs[d, s * 2 + quad]
                dp = dot_lanes(outs, v)
                pf = p.astype(F32)
                weighted = pf * dp
                total = jnp.sum(weighted, axis=-1, keepdims=True)
                ds = (weighted - pf * total).astype(BF)
                back_packed[rows, lanes] = (unstacked(dot(ds, k)) * HEAD_DIM**-0.5).astype(BF)
                back_packed[rows, pl.ds(512 + quad * 256, 256)] = dot_rows(ds, qs).astype(BF)
                back_packed[rows, pl.ds(1024 + quad * 256, 256)] = dot_rows(p, outs).astype(BF)
        for c in range(3):
            cols = pl.ds(c * 512, 512)
            scatter_rows(g, d, cols, dot_rows(normed[d], back_packed[:, cols]))
        back, gain, shift = ln_back(stream[d, 0], dot_lanes(back_packed[...], wq[d]), lnp[d, 0:1])
        lng[pl.ds(d * 4, 1), :] = gain
        lng[pl.ds(d * 4 + 2, 1), :] = shift
        up[...] += back
        return 0

    lax.fori_loop(0, layers, backward, 0)
    eg[...] = up[...].astype(BF)
    turned = jnp.transpose(lng[...]).astype(BF).reshape(8, 2, 32, 128)
    for core in range(2):
        gl[core] = turned[:, core]


def run_layers(tok, cot, lens, lnp, wq, wo, wu, wd):
    layers = wq.shape[0]
    vm = pl.BlockSpec(memory_space=pltpu.VMEM)
    sm = pl.BlockSpec(memory_space=pltpu.SMEM)
    hb = pl.BlockSpec(memory_space=pl.ANY)
    rows = 512
    return pl.pallas_call(
        layers_kernel,
        in_specs=[vm, vm, sm, vm, hb, hb, hb, hb],
        out_specs=[vm, vm, vm, vm],
        out_shape=[
            jax.ShapeDtypeStruct((2, 252, WIDTH), BF),
            jax.ShapeDtypeStruct((rows, WIDTH), BF),
            jax.ShapeDtypeStruct((layers, 2, 8, 32, LAYER_COLS), BF),
            jax.ShapeDtypeStruct((2, 8, 32, 128), BF),
        ],
        scratch_shapes=[
            pltpu.VMEM(wq.shape, BF),
            pltpu.VMEM(wo.shape, BF),
            pltpu.VMEM(wu.shape, BF),
            pltpu.VMEM(wd.shape, BF),
            pltpu.VMEM((layers + 1, 2, rows, WIDTH), F32),
            pltpu.VMEM((layers, rows, WIDTH), BF),
            pltpu.VMEM((layers, rows, 3 * WIDTH), BF),
            pltpu.VMEM((layers, 4, 1024, 256), BF),
            pltpu.VMEM((layers, rows, WIDTH), BF),
            pltpu.VMEM((layers, rows, WIDTH), BF),
            pltpu.VMEM((layers, rows, 4 * WIDTH), BF),
            pltpu.VMEM((layers, rows, 4 * WIDTH), BF),
            pltpu.VMEM((2, 256, 256), F32),
            pltpu.VMEM((rows, WIDTH), F32),
            pltpu.VMEM((rows, 4 * WIDTH), BF),
            pltpu.VMEM((rows, WIDTH), BF),
            pltpu.VMEM((rows, 3 * WIDTH), BF),
            pltpu.VMEM((128, WIDTH), F32),
            pltpu.SemaphoreType.DMA((layers, 4)),
        ],
        compiler_params=pltpu.CompilerParams(vmem_limit_bytes=VMEM_LIMIT),
        name="layers",
    )(tok, cot, lens, lnp, wq, wo, wu, wd)


def enc_bwd_kernel(eg, xl, blocks, g1, g2, w2, ids, e, dpool, bs, bf, acc2, acc1):
    step = pl.program_id(0)

    @pl.when(step == 0)
    def _():
        hot = jnp.where(iota((512, TABLE), 1) == ids[...], 1.0, 0.0).astype(BF)
        code = dot_rows(eg[...], hot[:, :POOL_AT + 96]).astype(BF)
        dpool[...] = dot_rows(hot[:, POOL_AT : POOL_AT + 96], eg[...])
        parts = code[:, :CODES].reshape(8, 2, 32, CODES)
        tail = code[:, CODES : CODES + 128].reshape(8, 2, 32, 128)
        for core in range(2):
            e[core, :, :, pl.ds(512, CODES)] = parts[:, core]
            e[core, :, :, pl.ds(1536, 128)] = tail[:, core]
        acc2[...] = jnp.zeros_like(acc2)
        acc1[...] = jnp.zeros_like(acc1)

    pooled = dpool[pl.ds(pl.multiple_of(step * 32, 32), 32), :][:FRAMES_BLOCK] * (1.0 / 64.0)
    wide = jnp.broadcast_to(pooled[:, None, :], (FRAMES_BLOCK, 8, WIDTH)).reshape(BLOCK_ROWS, WIDTH)

    def part(bx, _):
        rows = pl.ds(pl.multiple_of(bx * BLOCK_ROWS, BLOCK_ROWS), BLOCK_ROWS)
        back = (wide * g2[0, rows, :].astype(F32)).astype(BF)
        bs[rows, :] = back
        bf[rows, :] = (dot_lanes(back, w2[...]) * g1[0, rows, :].astype(F32)).astype(BF)
        return 0

    lax.fori_loop(0, 8, part, 0)
    acc2[...] += dot_rows(bs[...], blocks[0])
    for dy2 in range(2):
        acc1[:, pl.ds(dy2 * 256, 256)] += dot_rows(
            xl[0, :, pl.ds(dy2 * 128, 128)], bf[:, pl.ds(dy2 * 256, 256)]
        )

    @pl.when(step == pl.num_programs(0) - 1)
    def _():
        parts = acc2[...].astype(BF).reshape(8, 2, 32, WIDTH)
        both = acc1[:, pl.ds(0, 256)] + acc1[:, pl.ds(256, 256)]
        hot, rest = patch_index(128)
        first = jnp.where(rest[:, :1] < 12, both[:, :128], both[:, 128:])
        first = lax.dot_general(
            first, hot, (((0,), (0,)), ((), ())), preferred_element_type=F32,
            precision=lax.Precision.HIGHEST,
        )
        first = first.reshape(8, 2, 8, 48)
        first = jnp.concatenate([first, jnp.zeros((8, 2, 24, 48), F32)], axis=2).astype(BF)
        for core in range(2):
            e[core, :, :, pl.ds(0, WIDTH)] = parts[:, core]
            e[core, :, :, pl.ds(1536 + 64, 48)] = first[:, core]


def enc_backward(eg, xl, blocks, g1, g2, w2, ids):
    grid, rows, _ = xl.shape

    def whole(shape):
        return pl.BlockSpec(shape, lambda i: (0,) * len(shape))

    def saved(lanes):
        return pl.BlockSpec((1, rows, lanes), lambda i: (i, 0, 0))

    return pl.pallas_call(
        enc_bwd_kernel,
        grid=(grid,),
        in_specs=[
            whole(eg.shape), saved(256), saved(512), saved(512), saved(512),
            whole(w2.shape), whole(ids.shape),
        ],
        out_specs=whole((2, 8, 32, ENC_COLS)),
        out_shape=jax.ShapeDtypeStruct((2, 8, 32, ENC_COLS), BF),
        scratch_shapes=[
            pltpu.VMEM((96, WIDTH), F32),
            pltpu.VMEM((rows, WIDTH), BF),
            pltpu.VMEM((rows, WIDTH), BF),
            pltpu.VMEM((WIDTH, WIDTH), F32),
            pltpu.VMEM((128, WIDTH), F32),
        ],
        compiler_params=pltpu.CompilerParams(vmem_limit_bytes=VMEM_LIMIT),
        name="enc_bwd",
    )(eg, xl, blocks, g1, g2, w2, ids)


CHIPS = 8
HOPS = CHIPS - 1
MESH = pl.DeviceIdType.MESH


def ring_place(chip):
    z, x = chip // 2, chip % 2
    return z * (1 - x) + (7 - z) * x


def ring_chip(place):
    half = place // 4
    return (1 - half) * (2 * place) + half * (15 - 2 * place)


def where_am_i():
    section, me = lax.axis_index("section"), lax.axis_index("dp")
    core, chip = me % 2, me // 2
    place = ring_place(chip)
    ahead = ring_chip((place + 1) % CHIPS) * 2 + core
    behind = ring_chip((place + CHIPS - 1) % CHIPS) * 2 + core
    sibling = chip * 2 + (1 - core)
    return section, me, core, place, ahead, behind, sibling


def greet():
    section, me, _, _, ahead, behind, sibling = where_am_i()
    barrier = pltpu.get_barrier_semaphore()
    for target in ((section, sibling), (section, ahead), (section, behind), (1 - section, me)):
        pl.semaphore_signal(barrier, inc=1, device_id=target, device_id_type=MESH)
    pl.semaphore_wait(barrier, 4)


class Ring:
    def __init__(self, part, pair, hop, pair_sem, send_sem, recv_sem):
        self.part, self.pair, self.hop = part, pair, hop
        self.pair_sem, self.send_sem, self.recv_sem = pair_sem, send_sem, recv_sem

    def pair_copy(self):
        section, _, core, _, _, _, sibling = where_am_i()
        return pltpu.make_async_remote_copy(
            src_ref=self.part.at[1 - core], dst_ref=self.pair,
            send_sem=self.pair_sem.at[0], recv_sem=self.pair_sem.at[1],
            device_id=(section, sibling), device_id_type=MESH,
        )

    def target(self, way, step):
        place = where_am_i()[3]
        move = CHIPS - 1 - step if way == 0 else 1 + step
        return ring_chip((place + move) % CHIPS)

    def hop_copy(self, way, step):
        section, _, _, _, ahead, behind, _ = where_am_i()
        return pltpu.make_async_remote_copy(
            src_ref=self.pair.at[self.target(way, step), pl.ds(16 * way, 16)],
            dst_ref=self.hop.at[way, step],
            send_sem=self.send_sem.at[way, step], recv_sem=self.recv_sem.at[way, step],
            device_id=(section, ahead if way == 0 else behind), device_id_type=MESH,
        )

    def total(self, way, step, first):
        core = where_am_i()[2]
        at, rows = self.target(way, step), pl.ds(16 * way, 16)
        value = self.part[core, at, rows, :].astype(F32) + self.pair[at, rows, :].astype(F32)
        if not first:
            value += self.hop[way, step - 1].astype(F32)
        return value

    def start(self):
        self.pair_copy().start()

    def open(self):
        self.pair_copy().wait()
        for way in range(2):
            value = self.total(way, 0, True)
            self.pair[self.target(way, 0), pl.ds(16 * way, 16), :] = value.astype(BF)
            self.hop_copy(way, 0).start()

    def step(self, step):
        for way in range(2):
            self.hop_copy(way, step - 1).wait()
            value = self.total(way, step, False)
            self.pair[self.target(way, step), pl.ds(16 * way, 16), :] = value.astype(BF)
            self.hop_copy(way, step).start()

    def close(self, out):
        for way in range(2):
            self.hop_copy(way, HOPS - 1).wait()
            out[pl.ds(16 * way, 16), :] = self.total(way, HOPS, False).astype(out.dtype)


def cross_copy(src, dst, sem):
    section, me = lax.axis_index("section"), lax.axis_index("dp")
    return pltpu.make_async_remote_copy(
        src_ref=src, dst_ref=dst, send_sem=sem.at[0], recv_sem=sem.at[1],
        device_id=(1 - section, me), device_id_type=MESH,
    )


def sums_kernel(*refs):
    count = 4
    (g, gl, e), refs = refs[:3], refs[3:]
    parts = [g.at[1], g.at[0], gl, e]
    outs, refs = refs[:count], refs[count:]
    pairs, refs = refs[:count], refs[count:]
    hops, refs = refs[:count], refs[count:]
    mine, refs = refs[: count - 1], refs[count - 1 :]
    theirs, refs = refs[: count - 1], refs[count - 1 :]
    pair_sem, send_sem, recv_sem, cross_sem = refs
    greet()
    rings = [
        Ring(parts[k], pairs[k], hops[k], pair_sem.at[k], send_sem.at[k], recv_sem.at[k])
        for k in range(count)
    ]
    for ring in rings:
        ring.start()
    for ring in rings:
        ring.open()

    def hop(step, _):
        for ring in rings:
            ring.step(step)
        return 0

    lax.fori_loop(1, HOPS, hop, 0)
    crossings = []
    for k in range(count - 1):
        rings[k].close(mine[k])
        crossing = cross_copy(mine[k], theirs[k], cross_sem.at[k])
        crossing.start()
        crossings.append(crossing)
    rings[count - 1].close(outs[count - 1])
    for k in range(count - 1):
        crossings[k].wait()
        outs[k][...] = theirs[k][...]


def scatter_ring(g, gl, e):
    count = 4
    widths = [g.shape[-1], g.shape[-1], gl.shape[-1], e.shape[-1]]
    vm = pl.BlockSpec(memory_space=pltpu.VMEM)
    return pl.pallas_call(
        sums_kernel,
        in_specs=[vm] * 3,
        out_specs=[vm] * count,
        out_shape=[jax.ShapeDtypeStruct((32, n), BF) for n in widths],
        scratch_shapes=(
            [pltpu.VMEM((CHIPS, 32, n), BF) for n in widths]
            + [pltpu.VMEM((2, HOPS, 16, n), BF) for n in widths]
            + [pltpu.VMEM((32, n), BF) for n in widths[:-1]] * 2
            + [
                pltpu.SemaphoreType.DMA((count, 2)),
                pltpu.SemaphoreType.DMA((count, 2, HOPS)),
                pltpu.SemaphoreType.DMA((count, 2, HOPS)),
                pltpu.SemaphoreType.DMA((count - 1, 2)),
            ]
        ),
        compiler_params=pltpu.CompilerParams(
            collective_id=0, has_side_effects=True, vmem_limit_bytes=VMEM_LIMIT
        ),
        name="sums",
    )(g, gl, e)


def turn(rows):
    tall = jnp.concatenate([rows, jnp.zeros((96, rows.shape[1]), F32)], axis=0)
    return jnp.transpose(tall)[:, :32]


def outputs_kernel(late, early, norm, enc, qkv, out, up, down, gain, bias, bias2, enc1, enc2, book, acts):
    for d, rows in enumerate((early, late)):
        qkv[0, d] = rows[:, pl.ds(0, 1536)].astype(F32)
        out[0, d] = rows[:, pl.ds(1536, 512)].astype(F32)
        up[0, d] = rows[:, pl.ds(2048, 2048)].astype(F32)
        for j in range(4):
            down[0, d, pl.ds(32 * j, 32), :] = rows[:, pl.ds(4096 + 512 * j, 512)].astype(F32)
    turned = turn(norm[...].astype(F32))
    for d in range(2):
        gain[0, d] = norm[...].astype(F32)[:, 4 * d : 4 * d + 2]
        bias[0, pl.ds(d, 1)] = turned[4 * d + 2 : 4 * d + 3]
        bias2[0, pl.ds(d, 1)] = turned[4 * d + 3 : 4 * d + 4]
    enc2[0] = turn(enc[:, pl.ds(0, 512)].astype(F32))
    book[0] = turn(enc[:, pl.ds(512, 1024)].astype(F32))
    turned = turn(enc[:, pl.ds(1536, 128)].astype(F32))
    acts[0] = turned[:17]
    enc1[0] = turned[64:112, :8]


def spread_outputs(late, early, norm, enc):
    vm = pl.BlockSpec(memory_space=pltpu.VMEM)
    shapes = [
        (1, 2, 32, 1536), (1, 2, 32, 512), (1, 2, 32, 2048), (1, 2, 128, 512), (1, 2, 32, 2),
        (1, 2, 32), (1, 2, 32), (1, 48, 8), (1, 512, 32), (1, 1024, 32), (1, 17, 32),
    ]
    return pl.pallas_call(
        outputs_kernel,
        in_specs=[vm] * 4,
        out_specs=[vm] * len(shapes),
        out_shape=[jax.ShapeDtypeStruct(shape, F32) for shape in shapes],
        compiler_params=pltpu.CompilerParams(vmem_limit_bytes=VMEM_LIMIT),
        name="outputs",
    )(late, early, norm, enc)


def swap(array):
    return lax.ppermute(array, "section", [(0, 1), (1, 0)])


def whole_rows(g):
    return g.transpose(1, 0, 2, 3).reshape(512, g.shape[-1])


def scatter_plain(g, gl, e):
    def sums(array, axis):
        return lax.psum_scatter(array.astype(F32)[None], "dp", scatter_dimension=axis, tiled=True)

    layers = [whole_rows(g[d]) for d in range(g.shape[0])]
    qkv = jnp.stack([rows[:, :1536] for rows in layers])
    out = jnp.stack([rows[:, 1536:2048] for rows in layers])
    up = jnp.stack([rows[:, 2048:4096] for rows in layers])
    down = jnp.stack(
        [
            rows[:, 4096:].reshape(16, 32, 4, WIDTH).transpose(0, 2, 1, 3).reshape(2048, WIDTH)
            for rows in layers
        ]
    )
    norm = whole_rows(gl)[:, :8].reshape(512, 2, 4).transpose(1, 0, 2)
    enc = whole_rows(e)
    first = e.transpose(1, 0, 2, 3)[:, :, :8, 1600:1648].reshape(128, 48)
    layer_sums = [sums(x, 2) for x in (qkv, out, up, down, norm)]
    layer_sums = [swap(x) for x in layer_sums]
    norm = layer_sums.pop()
    return tuple(layer_sums) + (
        norm[..., 0:2],
        norm[..., 2],
        norm[..., 3],
        sums(first.T, 2),
        sums(enc[:, :512].T, 2),
        sums(enc[:, 512:1536].T, 2),
        sums(enc[:, 1536:1553].T, 2),
    )


def on_device(
    frames, action_ids, delta_ids, seq_len, enc_w1, enc_w2, codebook, action_table,
    ln_gain, ln_bias, w_qkv, w_out, w_up, w_down, cotangent,
):
    micro, steps = frames.shape[1], frames.shape[2]
    count = micro * steps
    frame = jnp.arange(count, dtype=I32).reshape(micro, steps, 1)
    pool_ids = POOL_AT + (frame // FRAMES_BLOCK) * 32 + frame % FRAMES_BLOCK
    ids = jnp.concatenate([pool_ids, action_ids[0][:, :, None] + ACT_AT, delta_ids[0]], axis=2)
    ids = ids.reshape(micro, steps * TPS)
    ids = jnp.pad(ids, ((0, 0), (0, 256 - steps * TPS)), constant_values=-1).reshape(512, 1)
    lnp = jnp.concatenate([ln_gain, ln_bias], axis=2).transpose(0, 2, 1)

    cot = swap(cotangent[0])
    tok, xl, blocks, g1, g2 = enc_forward(
        frames.reshape((count,) + frames.shape[3:]), enc_w1, enc_w2, codebook, action_table, ids
    )
    act, eg, g, gl = run_layers(tok, cot, seq_len, lnp, w_qkv, w_out, w_up, w_down)
    activations = swap(act)[None]
    embed_grad = eg.reshape(micro, 256, WIDTH)[None, :, : steps * TPS]
    e = enc_backward(eg, xl, blocks, g1, g2, enc_w2, ids)
    if lax.axis_size("dp") == 2 * CHIPS:
        late, early, norm, enc = scatter_ring(g, gl, e)
        return (activations, embed_grad) + tuple(spread_outputs(late, early, norm, enc))
    return (activations, embed_grad) + scatter_plain(g, gl, e)


def solution(mesh):
    return jax.shard_map(
        on_device,
        mesh=mesh,
        in_specs=(
            P("section", "dp", None, None, None),
            P("section", "dp", None),
            P("section", "dp", None, None),
            P(None, "dp"),
            P(), P(), P(), P(), P(), P(), P(), P(), P(), P(),
            P("section", "dp", None, None),
        ),
        out_specs=(
            P("section", "dp", None, None),
            P("section", "dp", None, None),
            P("section", None, "dp", None),
            P("section", None, "dp", None),
            P("section", None, "dp", None),
            P("section", None, "dp", None),
            P("section", None, "dp", None),
            P("section", None, "dp"),
            P("section", None, "dp"),
            P("section", None, "dp"),
            P("section", None, "dp"),
            P("section", None, "dp"),
            P("section", None, "dp"),
        ),
        check_vma=False,
    )
```

time: 1050 us -> 237 us (0.23); the launches traced: 1040 us -> 237 us
  waiting for transfers between devices: 543 us -> 0.01 us
  Pallas kernels: 0 us -> 217 us
  local copies, waits for them, and re-layouts: 192 us -> 14.4 us
  matrix products: 177 us -> 0 us
  blocking collectives: 58.2 us -> 0 us
  other arithmetic: 45.3 us -> 2.01 us
  between operations: 16.8 us -> 0.72 us
    reduce_scatter x4 -> x0, waiting for transfers between devices: 368 us -> none  [the longest x1 109 us: on_device(): lax.psum_scatter(local_up, 'dp', scatter_dimension=2, tiled=True)]
    pallas_call x0 -> x5, Pallas kernels: none -> 217 us  [the longest x1 99.2 us: scatter_ring(): pl.pallas_call(sums_kernel, in_specs=[vm] * 3, out_specs=[vm] * count, ou...]
    dot_general x45 -> x0, matrix products: 177 us -> none  [the longest x12 96.5 us: plain_dot(): return jnp.dot(operand, partner, preferred_element_type=jnp.float32)]
    unnamed x14 -> x0, waiting for transfers between devices: 158 us -> none
    reshape x15 -> x1, local copies, waits for them, and re-layouts: 66.6 us -> 0.12 us  [on_device(): ids = ids.reshape(micro, steps * TPS)]
    unnamed x1 -> x0, blocking collectives: 58.2 us -> none
    unnamed x169 -> x17, local copies, waits for them, and re-layouts: 55 us -> 14.1 us
    transpose x1 -> x0, local copies, waits for them, and re-layouts: 21.5 us -> none  [on_device(): patches = frames[0].reshape(frame_count, patch_grid, 4, patch_grid, 12).t...]
  transfers between devices with their start and end apart: 11 -> 2, of which waited for: 9 -> 0; matrix products, arithmetic and copies ran while one was open for 11% -> 6% of each run, Pallas kernels for 0% -> 66%
where the time goes in v1:
time: 237 us
  Pallas kernels  217 us (92%)
  local copies, waits for them, and re-layouts  14.4 us (6%)
  starting transfers between devices  3.12 us (1%)
    pallas_call x1, Pallas kernels, scatter_ring(): pl.pallas_call(sums_kernel, in_specs=[vm] * 3, out_specs=[vm] * count, ou...  99.2 us
    pallas_call x1, Pallas kernels, run_layers(): pl.pallas_call(layers_kernel, in_specs=[vm, vm, sm, vm, hb, hb, hb, hb],...  60.3 us
    pallas_call x1, Pallas kernels, enc_forward(): pl.pallas_call(enc_fwd_kernel, grid=(grid,), in_specs=[pl.BlockSpec((FRAM...  35.5 us
    pallas_call x1, Pallas kernels, enc_backward(): pl.pallas_call(enc_bwd_kernel, grid=(grid,), in_specs=[whole(eg.shape), s...  18.8 us
    unnamed x17, local copies, waits for them, and re-layouts  14.1 us
  transfers between devices with their start and end apart: 2, of which 0 were waited for; matrix products, arithmetic and copies ran while one was open for 6% of the time, Pallas kernels for 66%

profile of v1, /device:TPU:0, one launch (start us, length us, event | category | flops | bytes accessed | tf_op | source)
XLA Modules:
  0.0 236.7 jit_solution(2184441074765109789)
XLA Ops:
  0.6 0.0 copy-start.1
  0.7 0.0 copy-start.2
  0.7 1.1 copy.54
  1.8 3.0 %collective-permute-start = (bf16[2,252,512]{2,1,0:T(8,128)(2,1)S(1)}, bf16[2,252,512]{2,1,0:T(8,128)(2,1)S(1)}, u32[]{:S(2)}, u32[]{:S(2)}) collective-permute-start(bf16[2,252,512]{2,1,0:T(8,128)(2,1)S(1)} %bitcast.26), channel_id=1, source_target_pairs={{0,16},{16,0},{1,17},{17,1},{2,18},{18,2},{3,19},{19,3},{4,20},{20... | collective-permute-start | bytes 1548296 | tf_op jit(solution)/shard_map/ppermute | solution.py:683
  4.8 0.7 broadcast_add_fusion
  5.5 0.7 pad_add_fusion
  6.2 0.1 copy.38
  6.3 0.1 reshape.141
  6.5 0.9 copy.51
  7.3 35.5 %enc_fwd.1 = (bf16[512,512]{1,0:T(8,128)(2,1)}, bf16[3,1792,256]{2,1,0:T(8,128)(2,1)}, bf16[3,1792,512]{2,1,0:T(8,128)(2,1)}, bf16[3,1792,512]{2,1,0:T(8,128)(2,1)}, bf16[3,1792,512]{2,1,0:T(8,128)(2,1)}) custom-call(bf16[84,64,192]{2,1,0:T(8,128)(2,1)} %bitcast.21, bf16[48,128]{1,0:T(8,128)(2,1)} %w1.1, bf16[512,512]{1,0:T(8,128)(2,1)} %w2.3, ...), custom_call_target="tpu_custom_call" | custom-call | tf_op jit(solution)/shard_map/enc_fwd/pallas_call | solution.py:150
  42.8 0.0 copy-done.1
  42.8 0.0 copy-done.2
  42.8 0.6 maximum_bitcast_fusion.lnp
  43.5 0.0 collective-permute-done.cot
  43.5 0.0 copy-start
  43.5 0.8 copy-done
  44.2 60.3 %layers.1 = (bf16[2,252,512]{2,1,0:T(8,128)(2,1)}, bf16[512,512]{1,0:T(8,128)(2,1)}, bf16[2,2,8,32,6144]{4,3,2,1,0:T(8,128)(2,1)}, bf16[2,8,32,128]{3,2,1,0:T(8,128)(2,1)}) custom-call(bf16[512,512]{1,0:T(8,128)(2,1)} %get-tuple-element.37.tok, bf16[2,252,512]{2,1,0:T(8,128)(2,1)} %copy-done, s32[2,2]{1,0:T(2,128)} %lens.1, ...), custom_call_target="tpu_custom_call" | custom-call | tf_op jit(solution)/shard_map/layers/pallas_call | solution.py:362
  104.6 0.1 collective-permute-start.1
  104.7 2.4 copy.55
  107.0 18.8 %enc_bwd.1.refs_2_ = bf16[2,8,32,1664]{3,2,1,0:T(8,128)(2,1)} custom-call(bf16[512,512]{1,0:T(8,128)(2,1)} %get-tuple-element.39.eg, bf16[3,1792,256]{2,1,0:T(8,128)(2,1)} %get-tuple-element.42.xl, bf16[3,1792,512]{2,1,0:T(8,128)(2,1)} %get-tuple-element.43.blocks, bf16[3,1792,512]{2,1,0:T(8,128)(2,1)} %get-tuple-element.44.g1, ...), custom_call_target="tpu_custom_call" | custom-call | tf_op jit(solution)/shard_map/enc_bwd/pallas_call | solution.py:457
  125.8 99.2 %sums.1 = (bf16[32,6144]{1,0:T(8,128)(2,1)}, bf16[32,6144]{1,0:T(8,128)(2,1)}, bf16[32,128]{1,0:T(8,128)(2,1)}, bf16[32,1664]{1,0:T(8,128)(2,1)}) custom-call(bf16[2,2,8,32,6144]{4,3,2,1,0:T(8,128)(2,1)} %get-tuple-element.40.refs_0_, bf16[2,8,32,128]{3,2,1,0:T(8,128)(2,1)} %get-tuple-element.41.refs_1_, bf16[2,8,32,1664]{3,2,1,0:T(8,128)(2,1)} %enc_bwd.1.refs_2_), custom_call_target="tpu_custom_call" | custom-call | tf_op jit(solution)/shard_map/sums/pallas_call | solution.py:619
  225.0 2.7 %outputs.1 = (f32[1,2,32,1536]{3,2,1,0:T(8,128)}, f32[1,2,32,512]{3,2,1,0:T(8,128)}, f32[1,2,32,2048]{3,2,1,0:T(8,128)}, f32[1,2,128,512]{3,2,1,0:T(8,128)}, f32...) custom-call(bf16[32,6144]{1,0:T(8,128)(2,1)} %get-tuple-element.46.l, ...), custom_call_target="tpu_custom_call" | custom-call | tf_op jit(solution)/shard_map/outputs/pallas_call | solution.py:672
  227.7 1.4 copy.44
  229.1 1.4 copy.45
  230.5 1.3 copy.48
  231.9 1.7 copy.46
  233.5 1.9 copy.47
  235.4 0.0 collective-permute-done.1
  235.4 1.3 copy.43
  (3 shorter events, 0.0 us)
Async XLA Ops:
  0.6 42.2 %copy-start.1 = (f32[2,512,2]{1,2,0:T(2,128)S(1)}, f32[2,512,2]{1,2,0:T(2,128)}, u32[]{:S(2)}) copy-start(f32[2,512,2]{1,2,0:T(2,128)} %param.24) | copy-start | bytes 24580
  0.7 42.2 %copy-start.2 = (f32[2,512,2]{1,2,0:T(2,128)S(1)}, f32[2,512,2]{1,2,0:T(2,128)}, u32[]{:S(2)}) copy-start(f32[2,512,2]{1,2,0:T(2,128)} %param.23) | copy-start | bytes 24580
  1.8 41.7 %collective-permute-start = (bf16[2,252,512]{2,1,0:T(8,128)(2,1)S(1)}, bf16[2,252,512]{2,1,0:T(8,128)(2,1)S(1)}, u32[]{:S(2)}, u32[]{:S(2)}) collective-permute-start(bf16[2,252,512]{2,1,0:T(8,128)(2,1)S(1)} %bitcast.26), channel_id=1, source_target_pairs={{0,16},{16,0},{1,17},{17,1},{2,18},{18,2},{3,19},{19,3},{4,20},{20... | collective-permute-start | bytes 1548296 | tf_op jit(solution)/shard_map/ppermute | solution.py:683
  43.5 0.8 copy-start
  104.6 130.8 %collective-permute-start.1 = (bf16[2,252,512]{2,1,0:T(8,128)(2,1)}, bf16[2,252,512]{2,1,0:T(8,128)(2,1)S(1)}, u32[]{:S(2)}, u32[]{:S(2)}) collective-permute-start(bf16[2,252,512]{2,1,0:T(8,128)(2,1)} %get-tuple-element.38), channel_id=1, source_target_pairs={{0,16},{16,0},{1,17},{17,1},{2,18},{18,2},{3,19},{19,3},{4,20},{20... | collective-permute-start | bytes 1548296 | tf_op jit(solution)/shard_map/ppermute | solution.py:683

commit v2 on v1

--- a/solution.py
+++ b/solution.py
@@ -223,13 +223,21 @@
 
 
 def layers_kernel(
-    tok, cot, lens, lnp, wq_h, wo_h, wu_h, wd_h,
+    tok, cot_h, lens, lnp, wq_h, wo_h, wu_h, wd_h,
     act, eg, g, gl,
     wq, wo, wu, wd, stream, normed, packed, probs, att, normed2, gated, slope, bias,
-    up, back_up, back_att, back_packed, lng, sems,
+    up, back_up, back_att, back_packed, lng, cot, mine, theirs, sems, cross_sem,
 ):
     layers = wq.shape[0]
     section = lax.axis_index("section")
+    barrier = pltpu.get_barrier_semaphore()
+    pl.semaphore_signal(
+        barrier, inc=1, device_id=(1 - section, lax.axis_index("dp")), device_id_type=MESH
+    )
+    pl.semaphore_wait(barrier, 1)
+    cot_copy = cross_copy(cot_h, cot, cross_sem.at[0])
+    cot_copy.start()
+    act_copy = cross_copy(mine, theirs, cross_sem.at[1])
     copies = []
     for d in range(layers):
         for k, (src, dst) in enumerate(((wq_h, wq), (wo_h, wo), (wu_h, wu), (wd_h, wd))):
@@ -287,8 +295,10 @@
         return 0
 
     lax.fori_loop(0, layers, forward, 0)
+    cot_copy.wait()
+    mine[...] = stream[layers, 0].astype(BF)
+    act_copy.start()
     for s in range(2):
-        act[s] = stream[layers, 0, pl.ds(s * 256, 252), :].astype(BF)
         up[pl.ds(s * 256, 252), :] = cot[s].astype(F32)
         up[pl.ds(s * 256 + 252, 4), :] = jnp.zeros((4, WIDTH), F32)
     lng[...] = jnp.zeros_like(lng)
@@ -348,6 +358,9 @@
 
     lax.fori_loop(0, layers, backward, 0)
     eg[...] = up[...].astype(BF)
+    act_copy.wait()
+    for s in range(2):
+        act[s] = theirs[pl.ds(s * 256, 256), :].astype(F32)[:252].astype(BF)
     turned = jnp.transpose(lng[...]).astype(BF).reshape(8, 2, 32, 128)
     for core in range(2):
         gl[core] = turned[:, core]
@@ -361,7 +374,7 @@
     rows = 512
     return pl.pallas_call(
         layers_kernel,
-        in_specs=[vm, vm, sm, vm, hb, hb, hb, hb],
+        in_specs=[vm, hb, sm, vm, hb, hb, hb, hb],
         out_specs=[vm, vm, vm, vm],
         out_shape=[
             jax.ShapeDtypeStruct((2, 252, WIDTH), BF),
@@ -388,9 +401,15 @@
             pltpu.VMEM((rows, WIDTH), BF),
             pltpu.VMEM((rows, 3 * WIDTH), BF),
             pltpu.VMEM((128, WIDTH), F32),
+            pltpu.VMEM(cot.shape, BF),
+            pltpu.VMEM((rows, WIDTH), BF),
+            pltpu.VMEM((rows, WIDTH), BF),
             pltpu.SemaphoreType.DMA((layers, 4)),
+            pltpu.SemaphoreType.DMA((2, 2)),
         ],
-        compiler_params=pltpu.CompilerParams(vmem_limit_bytes=VMEM_LIMIT),
+        compiler_params=pltpu.CompilerParams(
+            collective_id=1, has_side_effects=True, vmem_limit_bytes=VMEM_LIMIT
+        ),
         name="layers",
     )(tok, cot, lens, lnp, wq, wo, wu, wd)
 
@@ -731,12 +750,11 @@
     ids = jnp.pad(ids, ((0, 0), (0, 256 - steps * TPS)), constant_values=-1).reshape(512, 1)
     lnp = jnp.concatenate([ln_gain, ln_bias], axis=2).transpose(0, 2, 1)
 
-    cot = swap(cotangent[0])
     tok, xl, blocks, g1, g2 = enc_forward(
         frames.reshape((count,) + frames.shape[3:]), enc_w1, enc_w2, codebook, action_table, ids
     )
-    act, eg, g, gl = run_layers(tok, cot, seq_len, lnp, w_qkv, w_out, w_up, w_down)
-    activations = swap(act)[None]
+    act, eg, g, gl = run_layers(tok, cotangent[0], seq_len, lnp, w_qkv, w_out, w_up, w_down)
+    activations = act[None]
     embed_grad = eg.reshape(micro, 256, WIDTH)[None, :, : steps * TPS]
     e = enc_backward(eg, xl, blocks, g1, g2, enc_w2, ids)
     if lax.axis_size("dp") == 2 * CHIPS:

time: 237 us -> 235 us (level)
  starting transfers between devices: 3.12 us -> 0 us
    ppermute x2 -> x0, starting transfers between devices: 3.12 us -> none  [swap(): return lax.ppermute(array, 'section', [(0, 1), (1, 0)])]
    pallas_call x1, Pallas kernels: 60.3 us -> 63.1 us  [run_layers(): pl.pallas_call(layers_kernel, in_specs=[vm, hb, sm, vm, hb, hb, hb, hb],...]
    unnamed x17 -> x15, local copies, waits for them, and re-layouts: 14.1 us -> 13.1 us
  transfers between devices with their start and end apart: 2 -> 0, of which waited for: 0 -> 0; matrix products, arithmetic and copies ran while one was open for 6% -> 0% of each run, Pallas kernels for 66% -> 0%
where the time goes in v2:
time: 235 us
  Pallas kernels  218 us (93%)
  local copies, waits for them, and re-layouts  13.3 us (6%)
  other arithmetic  2.73 us (1%)
    pallas_call x1, Pallas kernels, scatter_ring(): pl.pallas_call(sums_kernel, in_specs=[vm] * 3, out_specs=[vm] * count, ou...  97.8 us
    pallas_call x1, Pallas kernels, run_layers(): pl.pallas_call(layers_kernel, in_specs=[vm, hb, sm, vm, hb, hb, hb, hb],...  63.1 us
    pallas_call x1, Pallas kernels, enc_forward(): pl.pallas_call(enc_fwd_kernel, grid=(grid,), in_specs=[pl.BlockSpec((FRAM...  35.5 us
    pallas_call x1, Pallas kernels, enc_backward(): pl.pallas_call(enc_bwd_kernel, grid=(grid,), in_specs=[whole(eg.shape), s...  18.8 us
    unnamed x15, local copies, waits for them, and re-layouts  13.1 us

profile of v2, /device:TPU:0, one launch (start us, length us, event | category | flops | bytes accessed | tf_op | source)
XLA Modules:
  0.0 234.6 jit_solution(5118214995771001016)
XLA Ops:
  0.6 0.7 broadcast_add_fusion
  1.3 0.7 pad_add_fusion
  2.0 1.3 maximum_bitcast_fusion.lnp
  3.4 0.1 copy.38
  3.5 0.1 reshape.141
  3.6 0.9 copy.51
  4.5 1.9 copy.54
  6.4 35.5 %enc_fwd.1 = (bf16[512,512]{1,0:T(8,128)(2,1)}, bf16[3,1792,256]{2,1,0:T(8,128)(2,1)}, bf16[3,1792,512]{2,1,0:T(8,128)(2,1)}, bf16[3,1792,512]{2,1,0:T(8,128)(2,1)}, bf16[3,1792,512]{2,1,0:T(8,128)(2,1)}) custom-call(bf16[84,64,192]{2,1,0:T(8,128)(2,1)} %bitcast.21, bf16[48,128]{1,0:T(8,128)(2,1)} %w1.1, bf16[512,512]{1,0:T(8,128)(2,1)} %w2.3, ...), custom_call_target="tpu_custom_call" | custom-call | tf_op jit(solution)/shard_map/enc_fwd/pallas_call | solution.py:150
  41.9 63.1 %layers.1 = (bf16[2,252,512]{2,1,0:T(8,128)(2,1)}, bf16[512,512]{1,0:T(8,128)(2,1)}, bf16[2,2,8,32,6144]{4,3,2,1,0:T(8,128)(2,1)}, bf16[2,8,32,128]{3,2,1,0:T(8,128)(2,1)}) custom-call(bf16[512,512]{1,0:T(8,128)(2,1)} %get-tuple-element.37.tok, bf16[2,252,512]{2,1,0:T(8,128)(2,1)} %bitcast.25, s32[2,2]{1,0:T(2,128)} %lens.1, ...), custom_call_target="tpu_custom_call" | custom-call | tf_op jit(solution)/shard_map/layers/pallas_call | solution.py:375
  104.9 18.8 %enc_bwd.1.refs_2_ = bf16[2,8,32,1664]{3,2,1,0:T(8,128)(2,1)} custom-call(bf16[512,512]{1,0:T(8,128)(2,1)} %get-tuple-element.39.eg, bf16[3,1792,256]{2,1,0:T(8,128)(2,1)} %get-tuple-element.42.xl, bf16[3,1792,512]{2,1,0:T(8,128)(2,1)} %get-tuple-element.43.blocks, bf16[3,1792,512]{2,1,0:T(8,128)(2,1)} %get-tuple-element.44.g1, ...), custom_call_target="tpu_custom_call" | custom-call | tf_op jit(solution)/shard_map/enc_bwd/pallas_call | solution.py:476
  123.7 0.0 copy-start.1
  123.8 0.0 copy-start
  123.8 97.8 %sums.1 = (bf16[32,6144]{1,0:T(8,128)(2,1)}, bf16[32,6144]{1,0:T(8,128)(2,1)}, bf16[32,128]{1,0:T(8,128)(2,1)}, bf16[32,1664]{1,0:T(8,128)(2,1)}) custom-call(bf16[2,2,8,32,6144]{4,3,2,1,0:T(8,128)(2,1)} %get-tuple-element.40.refs_0_, bf16[2,8,32,128]{3,2,1,0:T(8,128)(2,1)} %get-tuple-element.41.refs_1_, bf16[2,8,32,1664]{3,2,1,0:T(8,128)(2,1)} %enc_bwd.1.refs_2_), custom_call_target="tpu_custom_call" | custom-call | tf_op jit(solution)/shard_map/sums/pallas_call | solution.py:638
  221.5 0.0 copy-done.1
  221.5 1.3 copy.43
  222.9 0.0 copy-done
  222.9 1.3 copy.55
  224.2 2.7 %outputs.1 = (f32[1,2,32,1536]{3,2,1,0:T(8,128)}, f32[1,2,32,512]{3,2,1,0:T(8,128)}, f32[1,2,32,2048]{3,2,1,0:T(8,128)}, f32[1,2,128,512]{3,2,1,0:T(8,128)}, f32...) custom-call(bf16[32,6144]{1,0:T(8,128)(2,1)} %get-tuple-element.46.l, ...), custom_call_target="tpu_custom_call" | custom-call | tf_op jit(solution)/shard_map/outputs/pallas_call | solution.py:691
  226.9 1.4 copy.44
  228.3 1.4 copy.45
  229.7 1.3 copy.48
  231.0 1.7 copy.46
  232.7 1.9 copy.47
  (3 shorter events, 0.0 us)
Async XLA Ops:
  123.7 97.8 %copy-start.1 = (bf16[2,252,512]{2,1,0:T(8,128)(2,1)S(1)}, bf16[2,252,512]{2,1,0:T(8,128)(2,1)}, u32[]{:S(2)}) copy-start(bf16[2,252,512]{2,1,0:T(8,128)(2,1)} %get-tuple-element.38) | copy-start | bytes 1548292
  123.8 99.1 %copy-start = (bf16[512,512]{1,0:T(8,128)(2,1)S(1)}, bf16[512,512]{1,0:T(8,128)(2,1)}, u32[]{:S(2)}) copy-start(bf16[512,512]{1,0:T(8,128)(2,1)} %get-tuple-element.39.eg) | copy-start | bytes 1572868
